TPU v7x, 128 devices: a whole 4x4x4 slice. The times are simulated.
128 devices in a mesh: pts: 64 (over z, y, x), head: 2 (over core).
Axes of the slice: x: 4, y: 4, z: 4, core: 2. Of those that a mesh axis runs over, the one named last changes fastest.
Arguments:
- points: bfloat16 [64, 262144], P(None, 'pts'), may hold values from -64 to 64
- counts: int32 [64], P('pts'), may hold values from 1 to 4096, 196608 in all
- latents_init: bfloat16 [512, 768], P('head'), may hold values from -6 to 6
- enc_key_w: bfloat16 [64, 768], replicated, may hold values from -0.75 to 0.75
- enc_val_w: bfloat16 [64, 768], replicated, may hold values from -0.75 to 0.75
- lat_weights: bfloat16 [7, 768, 768], P(None, 'head'), may hold values from -0.21875 to 0.21875
- up_w: bfloat16 [768, 3072], P(None, 'head'), may hold values from -0.21875 to 0.21875
- down_w: bfloat16 [3072, 768], P('head'), may hold values from -0.109375 to 0.109375
- query_w: bfloat16 [64, 768], replicated, may hold values from -0.75 to 0.75
- class_w: bfloat16 [768, 16], replicated, may hold values from -0.21875 to 0.21875
Outputs:
- logits: float32 [16, 262144], P(None, ('pts', 'head'))
Inputs may be any that keep to these rules, and one draw needn't show every extreme that they name: `counts`: every shard has at least one live point and one shard has exactly 4096.
All inputs are finite; a program needn't handle non-finite values.
Results may differ from a plain program's by a relative error of at most 0.025.
Values may be sent and summed in bfloat16 or wider, within the bound.
No kernel may reach another device: no remote copies, remote signals or barrier semaphores. Data moves between devices by JAX's collectives and lax.ppermute only.
A program may use at most 192 MiB of HBM per device.

v0:
```python
import math

import jax
import jax.numpy as jnp
from jax import lax
from jax.experimental import pallas as pl
from jax.experimental.pallas import tpu as pltpu
from jax.sharding import PartitionSpec as P

HEADS = 12
HSIZE = 64
WIDTH = HEADS * HSIZE
PAIRS = HEADS // 2
HALF = WIDTH // 2
KEY, VAL, QUERY, CLASS = 0, 64, 128, 192
OWNERS = 64
GROUPS = 32
LOG2_SCALE = HSIZE ** -0.5 * math.log2(math.e)
SAFE = 64.0
DEAD = -1e30

f32 = jnp.float32
bf16 = jnp.bfloat16
NT = (((1,), (1,)), ((), ()))
NN = (((1,), (0,)), ((), ()))


def dot(a, b, dims=NN):
    return lax.dot_general(a, b, dims, preferred_element_type=f32)


def norm(v):
    mean = jnp.mean(v, axis=-1, keepdims=True)
    cent = v - mean
    var = jnp.mean(cent * cent, axis=-1, keepdims=True)
    return cent * lax.rsqrt(var + 1e-05)


def split3(v):
    hi = v.astype(bf16).astype(f32)
    mid = (v - hi).astype(bf16).astype(f32)
    lo = (v - hi - mid).astype(bf16).astype(f32)
    return hi, mid, lo


def lanes(shape):
    return lax.broadcasted_iota(jnp.int32, shape, len(shape) - 1)


def block_diag(pair):
    lane = lanes(pair.shape)
    zero = jnp.zeros_like(pair)
    return jnp.concatenate([jnp.where(lane < 64, pair, zero), jnp.where(lane >= 64, pair, zero)], axis=0)


def vmem():
    return pl.BlockSpec(memory_space=pltpu.VMEM)


def smem():
    return pl.BlockSpec(memory_space=pltpu.SMEM)


def anywhere():
    return pl.BlockSpec(memory_space=pl.ANY)


def shape(dims, dtype=bf16):
    return jax.ShapeDtypeStruct(dims, dtype)


def params(mib=28):
    return pltpu.CompilerParams(vmem_limit_bytes=mib << 20)


def cost(flops, size, exps=0):
    return pl.CostEstimate(flops=flops, bytes_accessed=size, transcendentals=exps)


def prepare_kernel(count_ref, pts_ref, pack_ref, before, paug, pvt, normed, pn_ref):
    slots = pts_ref.shape[1]
    count = count_ref[0]
    sub = lax.broadcasted_iota(jnp.int32, (64, slots), 0)
    col = lanes((64, slots))
    ext = jnp.where(sub < 3, 1.0, jnp.where((sub == 3) & (col >= count), DEAD, 0.0))
    paug[0:64, :] = pts_ref[...]
    paug[64:128, :] = ext.astype(bf16)
    for i in range(slots // 128):
        blk = pts_ref[:, i * 128 : (i + 1) * 128].astype(f32)
        full = jnp.concatenate([blk, jnp.ones((64, 128), f32)], axis=0)
        pvt[i * 128 : (i + 1) * 128, :] = full.T.astype(bf16)
    normed[...] = norm(pack_ref[HALF:, :].astype(f32)).astype(bf16)
    pall = pts_ref[...].astype(f32)
    pn_ref[0] = jnp.max(jnp.sum(pall * pall, axis=0, keepdims=True))


def prepare(count, points, pack, before):
    slots = points.shape[1]
    return pl.pallas_call(
        prepare_kernel,
        out_shape=(shape((128, slots)), shape((slots, 128)), shape((pack.shape[0] - HALF, WIDTH)), shape((1,), f32)),
        in_specs=[smem(), vmem(), vmem(), anywhere()],
        out_specs=(vmem(), vmem(), vmem(), smem()),
        compiler_params=params(),
        cost_estimate=cost(0, 6 << 20),
        name="prepare",
    )(count, points, pack, before)


ROW_TILE = 768
TOP_ROWS = 256
PT_TILE = 512


def encode_kernel(pos_ref, par_ref, pn_ref, normed, pack_own, pack_oth, small, paug, pvt, out_ref, q_ref, qf, qaug, acc):
    rows = qaug.shape[1]
    slots = paug.shape[1]
    keep = par_ref[0]

    lo, hi = normed[:, :HALF], normed[:, HALF:]
    first = pos_ref[0] == 0
    equery = dot(jnp.where(first, lo, hi), pack_own[:HALF, :]) + dot(jnp.where(first, hi, lo), pack_oth[:HALF, :])
    equery = equery.astype(bf16)
    lane8 = lanes((GROUPS, 8, 128))
    aug = jnp.where(lane8 == 67, 1.0, 0.0)
    for p in range(PAIRS):
        cols = slice(p * 128, (p + 1) * 128)
        x = dot(equery[:, cols], block_diag(small[KEY : KEY + 64, cols]), NT) * LOG2_SCALE
        x8 = x.reshape(GROUPS, 8, 128)
        y8 = pltpu.roll(x, 64, 1).reshape(GROUPS, 8, 128)
        s, q = p // 3, p % 3
        qf[s, 0, :, q] = jnp.where(lane8 < 64, x8, aug)
        qf[s, 1, :, q] = jnp.where(lane8 < 64, y8, aug)
    qall = qf[...].reshape(2 * rows, 128)
    qaug[...] = qall.astype(bf16).reshape(2, rows, 128)

    sub = lax.broadcasted_iota(jnp.int32, (128, 128), 0)
    sums = dot((qall * qall).astype(bf16), jnp.where(sub < 64, 1.0, 0.0).astype(bf16))
    shifted = jnp.max(sums) * pn_ref[0] > SAFE * SAFE

    @pl.when(shifted)
    def _():
        def tile(t, _):
            per = rows // TOP_ROWS
            at = pl.ds(pl.multiple_of(lax.rem(t, per) * TOP_ROWS, TOP_ROWS), TOP_ROWS)
            qt = qaug[t // per, at, :]

            def chunk(j, top):
                start = pl.multiple_of(j * PT_TILE, PT_TILE)
                sc = dot(qt, paug[:, pl.ds(start, PT_TILE)])
                return jnp.maximum(top, jnp.max(sc, axis=1, keepdims=True))

            top = lax.fori_loop(0, slots // PT_TILE, chunk, jnp.full((TOP_ROWS, 1), DEAD, f32))
            hi, mid, lo = split3(top)
            lane = lanes((TOP_ROWS, 128))
            shift = jnp.where(lane == 64, hi, jnp.where(lane == 65, mid, lo))
            same = (lane < 64) | (lane > 66)
            qaug[t // per, at, :] = jnp.where(same, qt.astype(f32), -shift).astype(bf16)
            return 0

        lax.fori_loop(0, 2 * rows // TOP_ROWS, tile, 0)

    q_ref[...] = qaug[keep]
    attend(qaug.at[1 - keep], paug, pvt, out_ref, acc)


def attend(q_ref, paug, pvt, out_ref, acc):
    rows = q_ref.shape[0]
    slots = paug.shape[1]

    def tile(t, _):
        at = pl.ds(pl.multiple_of(t * ROW_TILE, ROW_TILE), ROW_TILE)
        qt = q_ref[at, :]
        total = jnp.zeros((ROW_TILE, 128), f32)
        for j in range(slots // PT_TILE):
            cols = slice(j * PT_TILE, (j + 1) * PT_TILE)
            ex = jnp.exp2(dot(qt, paug[:, cols])).astype(bf16)
            total = total + dot(ex, pvt[cols, :])
        acc[at, :] = total
        return 0

    lax.fori_loop(0, rows // ROW_TILE, tile, 0)

    sums = acc[...].reshape(2, GROUPS, 3, 8, 128)
    turned = pltpu.roll(acc[rows // 2 :, :], 64, 1).reshape(GROUPS, 3, 8, 128)
    lane = lanes((GROUPS, 8, 128))
    parts = [jnp.where(lane < 64, sums[0, :, q], turned[:, q]) for q in range(3)]
    extra = jnp.zeros((GROUPS, 8, 128), f32)
    for e in range(2):
        for q in range(3):
            extra = jnp.where(lane == 64 + 3 * e + q, sums[e, :, q], extra)
    out_ref[...] = jnp.concatenate(parts + [extra], axis=1).astype(bf16)

    shifts = -q_ref[...].astype(f32)
    at = lanes(shifts.shape)
    shifted = jnp.max(jnp.where((at >= 64) & (at < 67), jnp.abs(shifts), 0.0)) > 0.0

    @pl.when(shifted)
    def _():
        tiles = shifts.reshape(2, GROUPS, 3, 8, 128)
        more = extra
        for e in range(2):
            for q in range(3):
                for k in range(3):
                    one = tiles[e, :, q, :, 64 + k : 65 + k]
                    more = jnp.where(lane == 72 + 8 * k + 3 * e + q, one, more)
        out_ref[...] = jnp.concatenate(parts + [more], axis=1).astype(bf16)


def encode(pos, par, pn, normed, pack_own, pack_oth, small, paug, pvt):
    slots = paug.shape[1]
    rows = normed.shape[0] * HEADS // 2
    return pl.pallas_call(
        encode_kernel,
        out_shape=(shape((GROUPS, 32, 128)), shape((rows, 128))),
        in_specs=[smem()] * 3 + [vmem()] * 6,
        out_specs=(vmem(), vmem()),
        scratch_shapes=[
            pltpu.VMEM((2, 2, GROUPS, 3, 8, 128), f32),
            pltpu.VMEM((2, rows, 128), bf16),
            pltpu.VMEM((rows, 128), f32),
        ],
        compiler_params=params(),
        cost_estimate=cost(rows * slots * 1024, 6 << 20, rows * slots),
        name="encode",
    )(pos, par, pn, normed, pack_own, pack_oth, small, paug, pvt)


def encode_rest(queries, paug, pvt):
    rows, slots = queries.shape[0], paug.shape[1]
    return pl.pallas_call(
        attend,
        out_shape=shape((GROUPS, 32, 128)),
        in_specs=[vmem()] * 3,
        out_specs=vmem(),
        scratch_shapes=[pltpu.VMEM((rows, 128), f32)],
        compiler_params=params(),
        cost_estimate=cost(rows * slots * 1024, 6 << 20, rows * slots),
        name="encode_rest",
    )(queries, paug, pvt)


def pair_kernel(x_ref, y_ref, out_ref):
    xs = [x_ref[...].astype(f32), y_ref[...].astype(f32)]
    exts = [x[:, 24:32, :] for x in xs]
    lane = lanes(exts[0].shape)
    inside = (lane >= 72) & (lane < 96)
    flag = jnp.max(jnp.where(inside, jnp.maximum(jnp.abs(exts[0]), jnp.abs(exts[1])), 0.0))
    out_ref[...] = (xs[0] + xs[1]).astype(bf16)

    @pl.when(flag > 0.0)
    def _():
        shifts = [pltpu.roll(e, 128 - 8, 2) + pltpu.roll(e, 128 - 16, 2) + pltpu.roll(e, 128 - 24, 2) for e in exts]
        top = jnp.maximum(shifts[0], shifts[1])
        total = jnp.zeros(lane.shape, f32)
        parts = [jnp.zeros(lane.shape, f32) for _ in range(3)]
        here = (lane >= 64) & (lane < 70)
        for x, e, s in zip(xs, exts, shifts):
            wt = jnp.where(here, jnp.exp2(s - top), 0.0)
            total = total + e * wt
            for q in range(3):
                fac = jnp.where(lane < 64, wt[:, :, 64 + q : 65 + q], wt[:, :, 67 + q : 68 + q])
                parts[q] = parts[q] + x[:, q * 8 : (q + 1) * 8, :] * fac
        for k, part in enumerate(split3(jnp.where(here, top, 0.0))):
            total = total + pltpu.roll(part, 8 * (k + 1), 2)
        out_ref[...] = jnp.concatenate(parts + [total], axis=1).astype(bf16)


def pair(x, y):
    return pl.pallas_call(
        pair_kernel,
        out_shape=shape(x.shape),
        in_specs=[vmem()] * 2,
        out_specs=vmem(),
        compiler_params=params(),
        cost_estimate=cost(0, 1 << 20),
        name="pair",
    )(x, y)


def merge_kernel(x_ref, out_ref, both):
    x = x_ref[...].astype(f32)
    ext = x[:, 24:32, :]
    lane = lanes(ext.shape)
    flag = jnp.max(jnp.where((lane >= 72) & (lane < 96), jnp.abs(ext), 0.0))
    both[...] = jnp.sum(x, axis=0)

    @pl.when(flag > 0.0)
    def _():
        shift = pltpu.roll(ext, 128 - 8, 2) + pltpu.roll(ext, 128 - 16, 2) + pltpu.roll(ext, 128 - 24, 2)
        wt = jnp.exp2(shift - jnp.max(shift, axis=0, keepdims=True))
        wt = jnp.where((lane >= 64) & (lane < 70), wt, 0.0)
        both[24:32, :] = jnp.sum(ext * wt, axis=0)
        for q in range(3):
            fac = jnp.where(lane < 64, wt[:, :, 64 + q : 65 + q], wt[:, :, 67 + q : 68 + q])
            both[q * 8 : (q + 1) * 8, :] = jnp.sum(x[:, q * 8 : (q + 1) * 8, :] * fac, axis=0)

    low = lanes((8, 128)) < 64
    parts = []
    for q in range(3):
        tot = jnp.where(low, both[24:32, 64 + q : 65 + q], both[24:32, 67 + q : 68 + q])
        parts.append(both[q * 8 : (q + 1) * 8, :] / tot)
    mean = jnp.concatenate(parts, axis=0).astype(bf16)
    for k in range(out_ref.shape[0]):
        out_ref[k] = mean


def merge(parts, copies):
    return pl.pallas_call(
        merge_kernel,
        out_shape=shape((copies, 24, 128)),
        in_specs=[vmem()],
        out_specs=vmem(),
        scratch_shapes=[pltpu.VMEM((32, 128), f32)],
        compiler_params=params(),
        cost_estimate=cost(0, 1 << 20),
        name="merge",
    )(parts)


def latent_kernel(
    pos_ref, g_own, g_oth, pack_own, pack_oth, small,
    wl_own, wl_oth, up_own, up_oth, down_own, down_oth,
    at_ref, b_ref,
    enc, mix, wbuf, sem,
):
    rows = mix.shape[0]
    head = pos_ref[0]
    copies = {}
    for i in (2, 3, 1, 4, 5, 6):
        for k, (src, at) in enumerate(((wl_own, head), (wl_oth, 1 - head))):
            dst = wbuf.at[i - 1, pl.ds(pl.multiple_of(at * HALF, HALF), HALF)]
            copies[i, k] = pltpu.make_async_copy(src.at[i], dst, sem.at[i - 1, k])
            copies[i, k].start()
    for k, (g, pack) in enumerate(((g_own, pack_own), (g_oth, pack_oth))):
        mean = g[...].astype(f32).reshape(GROUPS, 2, 3, 8, 128)
        for p in range(PAIRS):
            cols = slice(p * 128, (p + 1) * 128)
            part = mean[:, p // 3, p % 3].reshape(rows, 128).astype(bf16)
            val = dot(part, block_diag(small[VAL : VAL + 64, cols]))
            enc[k * rows : (k + 1) * rows, cols] = (pack[HALF:, cols].astype(f32) + val).astype(bf16)
    block_in = norm(enc[...].astype(f32)).astype(bf16)

    def proj(x, i):
        for k in range(2):
            copies[i, k].wait()
        return dot(x, wbuf[i - 1])

    keys = proj(block_in, 2).astype(bf16)
    vals = proj(block_in, 3).astype(bf16)
    query = proj(block_in[:rows], 1).astype(bf16)
    ones = jnp.ones((2 * rows, 128), bf16)
    low = lanes((rows, 128)) < 64
    zero = jnp.zeros((rows, 128), bf16)
    for p in range(PAIRS):
        cols = slice(p * 128, (p + 1) * 128)
        qp = query[:, cols]
        both = jnp.concatenate([jnp.where(low, qp, zero), jnp.where(low, zero, qp)], axis=0)
        sc = dot(both, keys[:, cols], NT) * LOG2_SCALE
        ex = jnp.exp2(sc - jnp.max(sc, axis=-1, keepdims=True)).astype(bf16)
        res = dot(ex, jnp.concatenate([vals[:, cols], ones], axis=1))
        res = res[:, :128] / res[:, 128:]
        mix[:, cols] = jnp.where(low, res[:rows], res[rows:]).astype(bf16)
    latent2 = enc[:rows].astype(f32) + proj(mix[...], 4)
    mlp_in = norm(latent2).astype(bf16)
    hidden = []
    for up in (up_own, up_oth):
        x = dot(mlp_in, up[...])
        hid = 0.5 * x * (1.0 + jnp.tanh(math.sqrt(2.0 / math.pi) * (x + 0.044715 * (x * x * x))))
        hidden.append(hid.astype(bf16))
    latents_out = (latent2 + dot(hidden[0], down_own[...]) + dot(hidden[1], down_oth[...])).astype(bf16)
    dec_in = norm(latents_out.astype(f32)).astype(bf16)
    dkeys = proj(dec_in, 5).astype(bf16)
    for p in range(PAIRS):
        cols = slice(p * 128, (p + 1) * 128)
        at_ref[cols, :] = (dot(block_diag(small[QUERY : QUERY + 64, cols]), dkeys[:, cols], NT) * LOG2_SCALE).astype(bf16)
    dvals = proj(dec_in, 6).astype(bf16)
    classes = small[CLASS : CLASS + 16, :]
    lane = lanes(classes.shape)
    none = jnp.zeros_like(classes)
    blocks = [jnp.where((lane >= 64 * h) & (lane < 64 * h + 64), classes, none) for h in range(16)]
    b_ref[...] = dot(dvals, jnp.concatenate(blocks, axis=0), NT).astype(bf16)


def latent_block(pos, g_own, g_oth, pack_own, pack_oth, small, weights):
    rows = pack_own.shape[0] - HALF
    return pl.pallas_call(
        latent_kernel,
        out_shape=(shape((WIDTH, rows)), shape((rows, 256))),
        in_specs=[smem()] + [vmem()] * 5 + [anywhere()] * 2 + [vmem()] * 4,
        out_specs=(vmem(), vmem()),
        scratch_shapes=[
            pltpu.VMEM((2 * rows, WIDTH), bf16),
            pltpu.VMEM((rows, WIDTH), bf16),
            pltpu.VMEM((6, WIDTH, WIDTH), bf16),
            pltpu.SemaphoreType.DMA((6, 2)),
        ],
        compiler_params=params(),
        cost_estimate=cost(6 << 30, 20 << 20, 3 << 20),
        name="latent_block",
    )(pos, g_own, g_oth, pack_own, pack_oth, small, *weights)


DEC_TILE = 1024
TOP_TILE = 128


def decode_kernel(pos_ref, pn_ref, pts_ref, at_own, at_oth, b_own, b_oth, out_ref, pt, amat, bmat):
    share = out_ref.shape[1]
    rows = b_own.shape[0]
    for i in range(share // 128):
        start = pl.multiple_of(pos_ref[0] * share + i * 128, 128)
        blk = pts_ref[:, pl.ds(start, 128)].astype(f32)
        full = jnp.concatenate([blk, jnp.zeros((64, 128), f32)], axis=0)
        pt[i * 128 : (i + 1) * 128, :] = full.T.astype(bf16)
    sub = lax.broadcasted_iota(jnp.int32, (64, 2 * rows), 0)
    lane = lanes((rows, 128))
    worst = jnp.zeros((1, rows), f32)
    for h in range(HEADS):
        amat[h, 64:128, :] = jnp.where((sub >= 3 * h) & (sub < 3 * h + 3), 1.0, 0.0).astype(bf16)
        for k, (a, b) in enumerate(((at_own, b_own), (at_oth, b_oth))):
            part = a[h * 64 : (h + 1) * 64, :]
            amat[h, 0:64, k * rows : (k + 1) * rows] = part
            part = part.astype(f32)
            worst = jnp.maximum(worst, jnp.sum(part * part, axis=0, keepdims=True))
            g = h // 8
            own = (lane >= 16 * (h % 8)) & (lane < 16 * (h % 8) + 16)
            vals = b[:, g * 128 : (g + 1) * 128]
            bmat[h, k * rows : (k + 1) * rows, 0:128] = jnp.where(own, vals, jnp.zeros_like(vals))
            bmat[h, k * rows : (k + 1) * rows, 128:256] = jnp.ones((rows, 128), bf16)

    @pl.when(jnp.max(worst) * pn_ref[0] > SAFE * SAFE)
    def _():
        def tops(j, _):
            at = pl.ds(pl.multiple_of(j * TOP_TILE, TOP_TILE), TOP_TILE)
            pts = pt[at, :]
            new = pts.astype(f32)
            few = lanes((TOP_TILE, 128))
            for h in range(HEADS):
                top = jnp.max(dot(pts, amat[h]), axis=1, keepdims=True)
                for k, part in enumerate(split3(top)):
                    new = jnp.where(few == 64 + 3 * h + k, -part, new)
            pt[at, :] = new.astype(bf16)
            return 0

        lax.fori_loop(0, share // TOP_TILE, tops, 0)

    def block(j, _):
        at = pl.ds(pl.multiple_of(j * DEC_TILE, DEC_TILE), DEC_TILE)
        pts = pt[at, :]
        total = jnp.zeros((DEC_TILE, 128), f32)
        coming = dot(pts, amat[0])
        for h in range(HEADS):
            sc = coming
            if h + 1 < HEADS:
                coming = dot(pts, amat[h + 1])
            res = dot(jnp.exp2(sc).astype(bf16), bmat[h])
            total = total + res[:, :128] / res[:, 128:]
        for turn in (64, 32, 16):
            total = total + pltpu.roll(total, turn, 1)
        out_ref[:, at] = total.T[0:16, :]
        return 0

    lax.fori_loop(0, share // DEC_TILE, block, 0)


def decode(pos, pn, points, at_own, at_oth, b_own, b_oth):
    rows = b_own.shape[0]
    share = points.shape[1] // 2
    return pl.pallas_call(
        decode_kernel,
        out_shape=shape((16, share), f32),
        in_specs=[smem(), smem()] + [vmem()] * 5,
        out_specs=vmem(),
        scratch_shapes=[
            pltpu.VMEM((share, 128), bf16),
            pltpu.VMEM((HEADS, 128, 2 * rows), bf16),
            pltpu.VMEM((HEADS, 2 * rows, 256), bf16),
        ],
        compiler_params=params(),
        cost_estimate=cost(3 << 32, 8 << 20, 12 << 20),
        name="decode",
    )(pos, pn, points, at_own, at_oth, b_own, b_oth)


PARITIES = [list(range(k, OWNERS, 2)) for k in range(2)]


def per_device(
    points, counts, latents_init, enc_key_w, enc_val_w, lat_weights, up_w, down_w, query_w, class_w
):
    swap = [(0, 1), (1, 0)]

    def other(x):
        return lax.ppermute(x, "head", swap)

    pos = lax.axis_index("head").astype(jnp.int32).reshape(1)
    par = (lax.axis_index("pts") & 1).astype(jnp.int32).reshape(1)
    pos, par, lat_weights = lax.optimization_barrier((pos, par, lat_weights))
    pack_own = jnp.concatenate([lat_weights[0], latents_init], axis=0)
    pack_oth = other(pack_own)
    small = jnp.concatenate([enc_key_w, enc_val_w, query_w, class_w.T], axis=0)
    paug, pvt, normed, pn = prepare(counts, points, pack_own, small)
    (pn, pack_oth), late = lax.optimization_barrier(((pn, pack_oth), (lat_weights, up_w, down_w)))
    wl_oth, up_oth, down_oth = [other(w) for w in late]
    away, queries = encode(pos, par, pn, normed, pack_own, pack_oth, small, paug, pvt)
    came = lax.ppermute(away, "pts", [(i, i ^ 1) for i in range(OWNERS)])
    part = pair(encode_rest(queries, paug, pvt), came)

    parts = lax.all_to_all(part, "pts", 0, 0, axis_index_groups=PARITIES)
    g_own = lax.all_to_all(merge(parts, OWNERS), "pts", 0, 0)
    g_oth = other(g_own)

    weights = (lat_weights, wl_oth, up_w, up_oth, down_w, down_oth)
    at_own, b_own = latent_block(pos, g_own, g_oth, pack_own, pack_oth, small, weights)
    return decode(pos, pn, points, at_own, other(at_own), b_own, other(b_own))


def solution(mesh):
    placed = (
        P(None, "pts"),
        P("pts"),
        P("head", None),
        P(),
        P(),
        P(None, "head", None),
        P(None, "head"),
        P("head", None),
        P(),
        P(),
    )
    return jax.shard_map(
        per_device, mesh=mesh, in_specs=placed, out_specs=P(None, ("pts", "head")), check_vma=False
    )
```

profile of v0, /device:TPU:1, one launch (start us, length us, event | category | flops | bytes accessed | tf_op | source)
XLA Modules:
  0.0 138.5 jit_solution(2886260755681943138)
XLA Ops:
  0.0 1.2 slice_bitcast_fusion
  1.2 0.0 copy-start.1
  1.2 1.2 pad_maximum_fusion.pack_ref.pack_own
  2.4 1.5 %collective-permute-start = (bf16[640,768]{1,0:T(8,128)(2,1)S(1)}, bf16[640,768]{1,0:T(8,128)(2,1)S(1)}, u32[]{:S(2)}, u32[]{:S(2)}) collective-permute-start(bf16[640,768]{1,0:T(8,128)(2,1)S(1)} %pad_maximum_fusion.pack_ref.pack_own), channel_id=1, source_target_pairs={{0,1},{1,0},{2,3},{3,2},{4,5},{5,4},{6,7},{7,6},{8,9},{9,8},{10,11... | collective-permute-start | bytes 2949128 | tf_op jit(solution)/shard_map/ppermute | solution.py:495
  4.7 1.1 prepare.1
  5.8 0.3 collective-permute-done.pack_oth
  6.1 0.0 copy-done.1
  6.1 0.4 collective-permute-start.3
  6.5 0.1 collective-permute-start.4
  6.6 0.4 collective-permute-start.5
  7.0 39.5 %encode.1 = (bf16[32,32,128]{2,1,0:T(8,128)(2,1)S(1)}, bf16[1536,128]{1,0:T(8,128)(2,1)S(1)}) custom-call(s32[1]{0:T(128)} %bitcast.pos_ref, s32[1]{0:T(128)} %bitcast.1.par_ref, f32[1]{0:T(128)} %get-tuple-element.24.pn_ref, bf16[256,768]{1,0:T(8,128)(2,1)S(1)} %get-tuple-element.26.normed, bf16[640,768]{1,0:T(8,128)(2,1)S(1)} %pad_maximum_fusion.pack_ref.pack_own, ...), custom_call_target="tpu_custom_call" | custom-call | flops 6442450944 | bytes 6291456 | tf_op jit(solution)/shard_map/encode/pallas_call | solution.py:213
  46.6 1.4 %collective-permute-start.1 = (bf16[32,32,128]{2,1,0:T(8,128)(2,1)S(1)}, bf16[32,32,128]{2,1,0:T(8,128)(2,1)S(1)}, u32[]{:S(2)}, u32[]{:S(2)}) collective-permute-start(bf16[32,32,128]{2,1,0:T(8,128)(2,1)S(1)} %get-tuple-element.31), channel_id=1, source_target_pairs={{0,2},{2,0},{4,6},{6,4},{8,10},{10,8},{12,14},{14,12},{16,18},{18,... | collective-permute-start | bytes 786440 | tf_op jit(solution)/shard_map/ppermute | solution.py:507
  48.0 8.4 %encode_rest.1.x_ref = bf16[32,32,128]{2,1,0:T(8,128)(2,1)S(1)} custom-call(bf16[1536,128]{1,0:T(8,128)(2,1)S(1)} %get-tuple-element.30.q_ref, bf16[128,4096]{1,0:T(8,128)(2,1)S(1)} %get-tuple-element.28.paug, bf16[4096,128]{1,0:T(8,128)(2,1)S(1)} %get-tuple-element.29.pvt), custom_call_target="tpu_custom_call" | custom-call | flops 6442450944 | bytes 6291456 | tf_op jit(solution)/shard_map/encode_rest/pallas_call | solution.py:231
  56.4 0.0 copy-start.2
  56.4 0.0 collective-permute-done.1.y_ref
  56.4 0.9 pair.1
  57.3 20.3 %all_to_all.10.x_ref = bf16[32,32,128]{2,1,0:T(8,128)(2,1)S(1)} all-to-all(bf16[32,32,128]{2,1,0:T(8,128)(2,1)S(1)} %pair.1), channel_id=1, replica_groups={{0,4,8,12,16,20,24,28,32,36,40,44,48,52,56,60,64,68,72,76,80,84,88,92,9..., dimensions={0} | all-to-all | bytes 524288 | tf_op jit(solution)/shard_map/all_to_all | solution.py:510
  77.6 0.7 merge.1
  78.3 14.1 %all_to_all.11.g_own = bf16[64,24,128]{2,1,0:T(8,128)(2,1)S(1)} all-to-all(bf16[64,24,128]{2,1,0:T(8,128)(2,1)S(1)} %merge.1), channel_id=1, replica_groups=mesh['pts'=64,'head'=2] {'pts'}, dimensions={0} | all-to-all | bytes 786432 | tf_op jit(solution)/shard_map/all_to_all | solution.py:511
  92.3 2.9 %collective-permute-start.2 = (bf16[64,24,128]{2,1,0:T(8,128)(2,1)S(1)}, bf16[64,24,128]{2,1,0:T(8,128)(2,1)S(1)}, u32[]{:S(2)}, u32[]{:S(2)}) collective-permute-start(bf16[64,24,128]{2,1,0:T(8,128)(2,1)S(1)} %all_to_all.11.g_own), channel_id=1, source_target_pairs={{0,1},{1,0},{2,3},{3,2},{4,5},{5,4},{6,7},{7,6},{8,9},{9,8},{10,11... | collective-permute-start | bytes 1179656 | tf_op jit(solution)/shard_map/ppermute | solution.py:495
  95.2 1.3 collective-permute-done.2.g_oth
  96.6 0.0 collective-permute-done.4.up_oth
  96.6 0.0 collective-permute-done.5.down_oth
  96.6 0.0 collective-permute-done.3.wl_oth
  96.6 0.0 copy-done.3
  96.6 0.0 copy-done.2
  96.6 12.7 %latent_block.1 = (bf16[768,256]{1,0:T(8,128)(2,1)S(1)}, bf16[256,256]{1,0:T(8,128)(2,1)S(1)}) custom-call(s32[1]{0:T(128)} %bitcast.pos_ref, bf16[64,24,128]{2,1,0:T(8,128)(2,1)S(1)} %all_to_all.11.g_own, bf16[64,24,128]{2,1,0:T(8,128)(2,1)S(1)} %collective-permute-done.2.g_oth, bf16[640,768]{1,0:T(8,128)(2,1)S(1)} %pad_maximum_fusion.pack_ref.pack_own, ...), custom_call_target="tpu_custom_call" | custom-call | flops 6442450944 | bytes 20971520 | tf_op jit(solution)/shard_map/latent_block/pallas_call | solution.py:387
  109.4 0.4 collective-permute-start.6
  109.8 0.1 collective-permute-start.7
  109.9 1.4 %collective-permute-done.7.b_oth = bf16[256,256]{1,0:T(8,128)(2,1)S(1)} collective-permute-done((bf16[256,256]{1,0:T(8,128)(2,1)S(1)}, bf16[256,256]{1,0:T(8,128)(2,1)S(1)}, u32[]{:S(2)}, u32[]{:S(2)}) %collective-permute-start.7) | collective-permute-done | bytes 131104 | tf_op jit(solution)/shard_map/ppermute | solution.py:495
  111.3 0.0 collective-permute-done.6.at_oth
  111.3 27.1 %decode.1 = f32[16,2048]{1,0:T(8,128)} custom-call(s32[1]{0:T(128)} %bitcast.pos_ref, f32[1]{0:T(128)} %get-tuple-element.24.pn_ref, bf16[64,4096]{1,0:T(8,128)(2,1)S(1)} %copy-done, bf16[768,256]{1,0:T(8,128)(2,1)S(1)} %get-tuple-element.35.at_own, bf16[768,256]{1,0:T(8,128)(2,1)S(1)} %collective-permute-done.6.at_oth, ...), custom_call_target="tpu_custom_call" | custom-call | flops 12884901888 | bytes 8388608 | tf_op jit(solution)/shard_map/decode/pallas_call | solution.py:470
  (12 shorter events, 0.0 us)
Async XLA Ops:
  0.0 4.6 %copy-start.7 = (bf16[768,16]{0,1:T(8,128)(2,1)S(1)}, bf16[768,16]{0,1:T(8,128)(2,1)}, u32[]{:S(2)}) copy-start(bf16[768,16]{0,1:T(8,128)(2,1)} %param.19) | copy-start | bytes 73732
  0.0 4.6 %copy-start.4 = (bf16[64,768]{1,0:T(8,128)(2,1)S(1)}, bf16[64,768]{1,0:T(8,128)(2,1)}, u32[]{:S(2)}) copy-start(bf16[64,768]{1,0:T(8,128)(2,1)} %param.18) | copy-start | bytes 294916
  0.0 4.6 %copy-start.5 = (bf16[64,768]{1,0:T(8,128)(2,1)S(1)}, bf16[64,768]{1,0:T(8,128)(2,1)}, u32[]{:S(2)}) copy-start(bf16[64,768]{1,0:T(8,128)(2,1)} %param.14) | copy-start | bytes 294916
  0.0 4.6 %copy-start.6 = (bf16[64,768]{1,0:T(8,128)(2,1)S(1)}, bf16[64,768]{1,0:T(8,128)(2,1)}, u32[]{:S(2)}) copy-start(bf16[64,768]{1,0:T(8,128)(2,1)} %param.13) | copy-start | bytes 294916
  0.0 4.6 %copy-start = (bf16[64,4096]{1,0:T(8,128)(2,1)S(1)}, bf16[64,4096]{1,0:T(8,128)(2,1)}, u32[]{:S(2)}) copy-start(bf16[64,4096]{1,0:T(8,128)(2,1)} %pts_ref.3) | copy-start | bytes 1572868
  1.2 4.9 %copy-start.1 = (bf16[7,384,768]{2,1,0:T(8,128)(2,1)S(1)}, bf16[7,384,768]{2,1,0:T(8,128)(2,1)}, u32[]{:S(2)}) copy-start(bf16[7,384,768]{2,1,0:T(8,128)(2,1)} %wl_own) | copy-start | bytes 12386308
  2.4 3.7 %collective-permute-start = (bf16[640,768]{1,0:T(8,128)(2,1)S(1)}, bf16[640,768]{1,0:T(8,128)(2,1)S(1)}, u32[]{:S(2)}, u32[]{:S(2)}) collective-permute-start(bf16[640,768]{1,0:T(8,128)(2,1)S(1)} %pad_maximum_fusion.pack_ref.pack_own), channel_id=1, source_target_pairs={{0,1},{1,0},{2,3},{3,2},{4,5},{5,4},{6,7},{7,6},{8,9},{9,8},{10,11... | collective-permute-start | bytes 2949128 | tf_op jit(solution)/shard_map/ppermute | solution.py:495
  6.1 90.5 %collective-permute-start.3 = (bf16[7,384,768]{2,1,0:T(8,128)(2,1)S(1)}, bf16[7,384,768]{2,1,0:T(8,128)(2,1)S(1)}, u32[]{:S(2)}, u32[]{:S(2)}) collective-permute-start(bf16[7,384,768]{2,1,0:T(8,128)(2,1)S(1)} %copy-done.1), channel_id=1, source_target_pairs={{0,1},{1,0},{2,3},{3,2},{4,5},{5,4},{6,7},{7,6},{8,9},{9,8},{10,11... | collective-permute-start | bytes 12386312 | tf_op jit(solution)/shard_map/ppermute | solution.py:495
  6.5 90.1 %collective-permute-start.4 = (bf16[768,1536]{1,0:T(8,128)(2,1)}, bf16[768,1536]{1,0:T(8,128)(2,1)S(1)}, u32[]{:S(2)}, u32[]{:S(2)}) collective-permute-start(bf16[768,1536]{1,0:T(8,128)(2,1)} %up_own.1), channel_id=1, source_target_pairs={{0,1},{1,0},{2,3},{3,2},{4,5},{5,4},{6,7},{7,6},{8,9},{9,8},{10,11... | collective-permute-start | bytes 7077896 | tf_op jit(solution)/shard_map/ppermute | solution.py:495
  6.6 89.9 %collective-permute-start.5 = (bf16[1536,768]{1,0:T(8,128)(2,1)}, bf16[1536,768]{1,0:T(8,128)(2,1)S(1)}, u32[]{:S(2)}, u32[]{:S(2)}) collective-permute-start(bf16[1536,768]{1,0:T(8,128)(2,1)} %down_own.1), channel_id=1, source_target_pairs={{0,1},{1,0},{2,3},{3,2},{4,5},{5,4},{6,7},{7,6},{8,9},{9,8},{10,11... | collective-permute-start | bytes 7077896 | tf_op jit(solution)/shard_map/ppermute | solution.py:495
  46.6 9.8 %collective-permute-start.1 = (bf16[32,32,128]{2,1,0:T(8,128)(2,1)S(1)}, bf16[32,32,128]{2,1,0:T(8,128)(2,1)S(1)}, u32[]{:S(2)}, u32[]{:S(2)}) collective-permute-start(bf16[32,32,128]{2,1,0:T(8,128)(2,1)S(1)} %get-tuple-element.31), channel_id=1, source_target_pairs={{0,2},{2,0},{4,6},{6,4},{8,10},{10,8},{12,14},{14,12},{16,18},{18,... | collective-permute-start | bytes 786440 | tf_op jit(solution)/shard_map/ppermute | solution.py:507
  48.0 48.6 %copy-start.3 = (bf16[1536,768]{1,0:T(8,128)(2,1)S(1)}, bf16[1536,768]{1,0:T(8,128)(2,1)}, u32[]{:S(2)}) copy-start(bf16[1536,768]{1,0:T(8,128)(2,1)} %down_own.1) | copy-start | bytes 7077892
  56.4 40.2 %copy-start.2 = (bf16[768,1536]{1,0:T(8,128)(2,1)S(1)}, bf16[768,1536]{1,0:T(8,128)(2,1)}, u32[]{:S(2)}) copy-start(bf16[768,1536]{1,0:T(8,128)(2,1)} %up_own.1) | copy-start | bytes 7077892
  92.3 4.2 %collective-permute-start.2 = (bf16[64,24,128]{2,1,0:T(8,128)(2,1)S(1)}, bf16[64,24,128]{2,1,0:T(8,128)(2,1)S(1)}, u32[]{:S(2)}, u32[]{:S(2)}) collective-permute-start(bf16[64,24,128]{2,1,0:T(8,128)(2,1)S(1)} %all_to_all.11.g_own), channel_id=1, source_target_pairs={{0,1},{1,0},{2,3},{3,2},{4,5},{5,4},{6,7},{7,6},{8,9},{9,8},{10,11... | collective-permute-start | bytes 1179656 | tf_op jit(solution)/shard_map/ppermute | solution.py:495
  109.4 2.0 %collective-permute-start.6 = (bf16[768,256]{1,0:T(8,128)(2,1)S(1)}, bf16[768,256]{1,0:T(8,128)(2,1)S(1)}, u32[]{:S(2)}, u32[]{:S(2)}) collective-permute-start(bf16[768,256]{1,0:T(8,128)(2,1)S(1)} %get-tuple-element.35.at_own), channel_id=1, source_target_pairs={{0,1},{1,0},{2,3},{3,2},{4,5},{5,4},{6,7},{7,6},{8,9},{9,8},{10,11... | collective-permute-start | bytes 1179656 | tf_op jit(solution)/shard_map/ppermute | solution.py:495
  109.8 1.5 %collective-permute-start.7 = (bf16[256,256]{1,0:T(8,128)(2,1)S(1)}, bf16[256,256]{1,0:T(8,128)(2,1)S(1)}, u32[]{:S(2)}, u32[]{:S(2)}) collective-permute-start(bf16[256,256]{1,0:T(8,128)(2,1)S(1)} %get-tuple-element.36.b_own), channel_id=1, source_target_pairs={{0,1},{1,0},{2,3},{3,2},{4,5},{5,4},{6,7},{7,6},{8,9},{9,8},{10,11... | collective-permute-start | bytes 393224 | tf_op jit(solution)/shard_map/ppermute | solution.py:495
where the time goes:
time: 139 us; the launch traced here: 138 us
  Pallas kernels  90.5 us (65%)
  blocking collectives  34.4 us (25%)
  starting transfers between devices  7.25 us (5%)
  waiting for transfers between devices  3.08 us (2%)
    pallas_call x1, Pallas kernels, encode(): pl.pallas_call(encode_kernel, out_shape=(shape((GROUPS, 32, 128)), shape(...  39.5 us
    pallas_call x1, Pallas kernels, decode(): pl.pallas_call(decode_kernel, out_shape=shape((16, share), f32), in_specs...  27.1 us
    all_to_all x1, blocking collectives, per_device(): parts = lax.all_to_all(part, 'pts', 0, 0, axis_index_groups=PARITIES)  20.3 us
    all_to_all x1, blocking collectives, per_device(): g_own = lax.all_to_all(merge(parts, OWNERS), 'pts', 0, 0)  14.1 us
    pallas_call x1, Pallas kernels, latent_block(): pl.pallas_call(latent_kernel, out_shape=(shape((WIDTH, rows)), shape((row...  12.7 us
    pallas_call x1, Pallas kernels, encode_rest(): pl.pallas_call(attend, out_shape=shape((GROUPS, 32, 128)), in_specs=[vmem...  8.41 us
    ppermute x7, starting transfers between devices, other(): return lax.ppermute(x, 'head', swap)  5.86 us
    ppermute x7, waiting for transfers between devices, other(): return lax.ppermute(x, 'head', swap)  3.08 us
  transfers between devices with their start and end apart: 8, of which 3 were waited for; matrix products, arithmetic and copies ran while one was open for 0% of the time, Pallas kernels for 37%

commit v1 on v0

--- a/solution.py
+++ b/solution.py
@@ -107,7 +107,7 @@
     )(count, points, pack, before)
 
 
-ROW_TILE = 768
+PT_TURN = 4 * 512
 TOP_ROWS = 256
 PT_TILE = 512
 
@@ -167,19 +167,19 @@
 def attend(q_ref, paug, pvt, out_ref, acc):
     rows = q_ref.shape[0]
     slots = paug.shape[1]
-
-    def tile(t, _):
-        at = pl.ds(pl.multiple_of(t * ROW_TILE, ROW_TILE), ROW_TILE)
-        qt = q_ref[at, :]
-        total = jnp.zeros((ROW_TILE, 128), f32)
-        for j in range(slots // PT_TILE):
-            cols = slice(j * PT_TILE, (j + 1) * PT_TILE)
+    qt = q_ref[...]
+    acc[...] = jnp.zeros(acc.shape, f32)
+
+    def turn(t, _):
+        total = acc[...]
+        for j in range(PT_TURN // PT_TILE):
+            cols = pl.ds(pl.multiple_of(t * PT_TURN + j * PT_TILE, PT_TILE), PT_TILE)
             ex = jnp.exp2(dot(qt, paug[:, cols])).astype(bf16)
             total = total + dot(ex, pvt[cols, :])
-        acc[at, :] = total
+        acc[...] = total
         return 0
 
-    lax.fori_loop(0, rows // ROW_TILE, tile, 0)
+    lax.fori_loop(0, slots // PT_TURN, turn, 0)
 
     sums = acc[...].reshape(2, GROUPS, 3, 8, 128)
     turned = pltpu.roll(acc[rows // 2 :, :], 64, 1).reshape(GROUPS, 3, 8, 128)

time: 139 us -> 138 us (level)
  transfers between devices with their start and end apart: 8 -> 8, of which waited for: 3 -> 3; matrix products, arithmetic and copies ran while one was open for 0% -> 0% of each run, Pallas kernels for 37% -> 36%
where the time goes in v1:
time: 138 us
  Pallas kernels  90 us (65%)
  blocking collectives  34.4 us (25%)
  starting transfers between devices  7.25 us (5%)
  waiting for transfers between devices  3.09 us (2%)
    pallas_call x1, Pallas kernels, encode(): pl.pallas_call(encode_kernel, out_shape=(shape((GROUPS, 32, 128)), shape(...  39.2 us
    pallas_call x1, Pallas kernels, decode(): pl.pallas_call(decode_kernel, out_shape=shape((16, share), f32), in_specs...  27.1 us
    all_to_all x1, blocking collectives, per_device(): parts = lax.all_to_all(part, 'pts', 0, 0, axis_index_groups=PARITIES)  20.3 us
    all_to_all x1, blocking collectives, per_device(): g_own = lax.all_to_all(merge(parts, OWNERS), 'pts', 0, 0)  14.1 us
    pallas_call x1, Pallas kernels, latent_block(): pl.pallas_call(latent_kernel, out_shape=(shape((WIDTH, rows)), shape((row...  12.7 us
    pallas_call x1, Pallas kernels, encode_rest(): pl.pallas_call(attend, out_shape=shape((GROUPS, 32, 128)), in_specs=[vmem...  8.17 us
    ppermute x7, starting transfers between devices, other(): return lax.ppermute(x, 'head', swap)  5.85 us
    ppermute x7, waiting for transfers between devices, other(): return lax.ppermute(x, 'head', swap)  3.09 us
  transfers between devices with their start and end apart: 8, of which 3 were waited for; matrix products, arithmetic and copies ran while one was open for 0% of the time, Pallas kernels for 36%

profile of v1, /device:TPU:1, one launch (start us, length us, event | category | flops | bytes accessed | tf_op | source)
XLA Modules:
  0.0 137.9 jit_solution(12654134748582960371)
XLA Ops:
  0.0 1.2 slice_bitcast_fusion
  1.2 0.0 copy-start.1
  1.2 1.2 pad_maximum_fusion.pack_ref.pack_own
  2.4 1.5 %collective-permute-start = (bf16[640,768]{1,0:T(8,128)(2,1)S(1)}, bf16[640,768]{1,0:T(8,128)(2,1)S(1)}, u32[]{:S(2)}, u32[]{:S(2)}) collective-permute-start(bf16[640,768]{1,0:T(8,128)(2,1)S(1)} %pad_maximum_fusion.pack_ref.pack_own), channel_id=1, source_target_pairs={{0,1},{1,0},{2,3},{3,2},{4,5},{5,4},{6,7},{7,6},{8,9},{9,8},{10,11... | collective-permute-start | bytes 2949128 | tf_op jit(solution)/shard_map/ppermute | solution.py:495
  4.6 0.0 copy-done.7
  4.6 0.0 copy-done.4
  4.6 0.0 copy-done.5
  4.7 1.1 prepare.1
  5.8 0.3 collective-permute-done.pack_oth
  6.1 0.4 collective-permute-start.3
  6.5 0.1 collective-permute-start.4
  6.6 0.4 collective-permute-start.5
  7.0 39.2 %encode.1 = (bf16[32,32,128]{2,1,0:T(8,128)(2,1)S(1)}, bf16[1536,128]{1,0:T(8,128)(2,1)S(1)}) custom-call(s32[1]{0:T(128)} %bitcast.pos_ref, s32[1]{0:T(128)} %bitcast.1.par_ref, f32[1]{0:T(128)} %get-tuple-element.24.pn_ref, bf16[256,768]{1,0:T(8,128)(2,1)S(1)} %get-tuple-element.26.normed, bf16[640,768]{1,0:T(8,128)(2,1)S(1)} %pad_maximum_fusion.pack_ref.pack_own, ...), custom_call_target="tpu_custom_call" | custom-call | flops 6442450944 | bytes 6291456 | tf_op jit(solution)/shard_map/encode/pallas_call | solution.py:213
  46.3 1.4 %collective-permute-start.1 = (bf16[32,32,128]{2,1,0:T(8,128)(2,1)S(1)}, bf16[32,32,128]{2,1,0:T(8,128)(2,1)S(1)}, u32[]{:S(2)}, u32[]{:S(2)}) collective-permute-start(bf16[32,32,128]{2,1,0:T(8,128)(2,1)S(1)} %get-tuple-element.31), channel_id=1, source_target_pairs={{0,2},{2,0},{4,6},{6,4},{8,10},{10,8},{12,14},{14,12},{16,18},{18,... | collective-permute-start | bytes 786440 | tf_op jit(solution)/shard_map/ppermute | solution.py:507
  47.7 8.2 %encode_rest.1.x_ref = bf16[32,32,128]{2,1,0:T(8,128)(2,1)S(1)} custom-call(bf16[1536,128]{1,0:T(8,128)(2,1)S(1)} %get-tuple-element.30.q_ref, bf16[128,4096]{1,0:T(8,128)(2,1)S(1)} %get-tuple-element.28.paug, bf16[4096,128]{1,0:T(8,128)(2,1)S(1)} %get-tuple-element.29.pvt), custom_call_target="tpu_custom_call" | custom-call | flops 6442450944 | bytes 6291456 | tf_op jit(solution)/shard_map/encode_rest/pallas_call | solution.py:231
  55.8 0.0 copy-start.2
  55.9 0.0 collective-permute-done.1.y_ref
  55.9 0.9 pair.1
  56.8 20.3 %all_to_all.10.x_ref = bf16[32,32,128]{2,1,0:T(8,128)(2,1)S(1)} all-to-all(bf16[32,32,128]{2,1,0:T(8,128)(2,1)S(1)} %pair.1), channel_id=1, replica_groups={{0,4,8,12,16,20,24,28,32,36,40,44,48,52,56,60,64,68,72,76,80,84,88,92,9..., dimensions={0} | all-to-all | bytes 524288 | tf_op jit(solution)/shard_map/all_to_all | solution.py:510
  77.1 0.7 merge.1
  77.7 14.1 %all_to_all.11.g_own = bf16[64,24,128]{2,1,0:T(8,128)(2,1)S(1)} all-to-all(bf16[64,24,128]{2,1,0:T(8,128)(2,1)S(1)} %merge.1), channel_id=1, replica_groups=mesh['pts'=64,'head'=2] {'pts'}, dimensions={0} | all-to-all | bytes 786432 | tf_op jit(solution)/shard_map/all_to_all | solution.py:511
  91.8 2.9 %collective-permute-start.2 = (bf16[64,24,128]{2,1,0:T(8,128)(2,1)S(1)}, bf16[64,24,128]{2,1,0:T(8,128)(2,1)S(1)}, u32[]{:S(2)}, u32[]{:S(2)}) collective-permute-start(bf16[64,24,128]{2,1,0:T(8,128)(2,1)S(1)} %all_to_all.11.g_own), channel_id=1, source_target_pairs={{0,1},{1,0},{2,3},{3,2},{4,5},{5,4},{6,7},{7,6},{8,9},{9,8},{10,11... | collective-permute-start | bytes 1179656 | tf_op jit(solution)/shard_map/ppermute | solution.py:495
  94.7 1.3 collective-permute-done.2.g_oth
  96.0 0.0 collective-permute-done.4.up_oth
  96.0 0.0 collective-permute-done.5.down_oth
  96.0 0.0 collective-permute-done.3.wl_oth
  96.1 12.7 %latent_block.1 = (bf16[768,256]{1,0:T(8,128)(2,1)S(1)}, bf16[256,256]{1,0:T(8,128)(2,1)S(1)}) custom-call(s32[1]{0:T(128)} %bitcast.pos_ref, bf16[64,24,128]{2,1,0:T(8,128)(2,1)S(1)} %all_to_all.11.g_own, bf16[64,24,128]{2,1,0:T(8,128)(2,1)S(1)} %collective-permute-done.2.g_oth, bf16[640,768]{1,0:T(8,128)(2,1)S(1)} %pad_maximum_fusion.pack_ref.pack_own, ...), custom_call_target="tpu_custom_call" | custom-call | flops 6442450944 | bytes 20971520 | tf_op jit(solution)/shard_map/latent_block/pallas_call | solution.py:387
  108.8 0.5 collective-permute-start.6
  109.3 0.1 collective-permute-start.7
  109.4 1.4 %collective-permute-done.7.b_oth = bf16[256,256]{1,0:T(8,128)(2,1)S(1)} collective-permute-done((bf16[256,256]{1,0:T(8,128)(2,1)S(1)}, bf16[256,256]{1,0:T(8,128)(2,1)S(1)}, u32[]{:S(2)}, u32[]{:S(2)}) %collective-permute-start.7) | collective-permute-done | bytes 131104 | tf_op jit(solution)/shard_map/ppermute | solution.py:495
  110.8 0.0 collective-permute-done.6.at_oth
  110.8 27.1 %decode.1 = f32[16,2048]{1,0:T(8,128)} custom-call(s32[1]{0:T(128)} %bitcast.pos_ref, f32[1]{0:T(128)} %get-tuple-element.24.pn_ref, bf16[64,4096]{1,0:T(8,128)(2,1)S(1)} %copy-done, bf16[768,256]{1,0:T(8,128)(2,1)S(1)} %get-tuple-element.35.at_own, bf16[768,256]{1,0:T(8,128)(2,1)S(1)} %collective-permute-done.6.at_oth, ...), custom_call_target="tpu_custom_call" | custom-call | flops 12884901888 | bytes 8388608 | tf_op jit(solution)/shard_map/decode/pallas_call | solution.py:470
  (12 shorter events, 0.0 us)
Async XLA Ops:
  0.0 4.6 %copy-start.7 = (bf16[768,16]{0,1:T(8,128)(2,1)S(1)}, bf16[768,16]{0,1:T(8,128)(2,1)}, u32[]{:S(2)}) copy-start(bf16[768,16]{0,1:T(8,128)(2,1)} %param.19) | copy-start | bytes 73732
  0.0 4.6 %copy-start.4 = (bf16[64,768]{1,0:T(8,128)(2,1)S(1)}, bf16[64,768]{1,0:T(8,128)(2,1)}, u32[]{:S(2)}) copy-start(bf16[64,768]{1,0:T(8,128)(2,1)} %param.18) | copy-start | bytes 294916
  0.0 4.6 %copy-start.5 = (bf16[64,768]{1,0:T(8,128)(2,1)S(1)}, bf16[64,768]{1,0:T(8,128)(2,1)}, u32[]{:S(2)}) copy-start(bf16[64,768]{1,0:T(8,128)(2,1)} %param.14) | copy-start | bytes 294916
  0.0 4.6 %copy-start.6 = (bf16[64,768]{1,0:T(8,128)(2,1)S(1)}, bf16[64,768]{1,0:T(8,128)(2,1)}, u32[]{:S(2)}) copy-start(bf16[64,768]{1,0:T(8,128)(2,1)} %param.13) | copy-start | bytes 294916
  0.0 4.6 %copy-start = (bf16[64,4096]{1,0:T(8,128)(2,1)S(1)}, bf16[64,4096]{1,0:T(8,128)(2,1)}, u32[]{:S(2)}) copy-start(bf16[64,4096]{1,0:T(8,128)(2,1)} %pts_ref.3) | copy-start | bytes 1572868
  1.2 4.9 %copy-start.1 = (bf16[7,384,768]{2,1,0:T(8,128)(2,1)S(1)}, bf16[7,384,768]{2,1,0:T(8,128)(2,1)}, u32[]{:S(2)}) copy-start(bf16[7,384,768]{2,1,0:T(8,128)(2,1)} %wl_own) | copy-start | bytes 12386308
  2.4 3.7 %collective-permute-start = (bf16[640,768]{1,0:T(8,128)(2,1)S(1)}, bf16[640,768]{1,0:T(8,128)(2,1)S(1)}, u32[]{:S(2)}, u32[]{:S(2)}) collective-permute-start(bf16[640,768]{1,0:T(8,128)(2,1)S(1)} %pad_maximum_fusion.pack_ref.pack_own), channel_id=1, source_target_pairs={{0,1},{1,0},{2,3},{3,2},{4,5},{5,4},{6,7},{7,6},{8,9},{9,8},{10,11... | collective-permute-start | bytes 2949128 | tf_op jit(solution)/shard_map/ppermute | solution.py:495
  6.1 89.9 %collective-permute-start.3 = (bf16[7,384,768]{2,1,0:T(8,128)(2,1)S(1)}, bf16[7,384,768]{2,1,0:T(8,128)(2,1)S(1)}, u32[]{:S(2)}, u32[]{:S(2)}) collective-permute-start(bf16[7,384,768]{2,1,0:T(8,128)(2,1)S(1)} %copy-done.1), channel_id=1, source_target_pairs={{0,1},{1,0},{2,3},{3,2},{4,5},{5,4},{6,7},{7,6},{8,9},{9,8},{10,11... | collective-permute-start | bytes 12386312 | tf_op jit(solution)/shard_map/ppermute | solution.py:495
  6.5 89.5 %collective-permute-start.4 = (bf16[768,1536]{1,0:T(8,128)(2,1)}, bf16[768,1536]{1,0:T(8,128)(2,1)S(1)}, u32[]{:S(2)}, u32[]{:S(2)}) collective-permute-start(bf16[768,1536]{1,0:T(8,128)(2,1)} %up_own.1), channel_id=1, source_target_pairs={{0,1},{1,0},{2,3},{3,2},{4,5},{5,4},{6,7},{7,6},{8,9},{9,8},{10,11... | collective-permute-start | bytes 7077896 | tf_op jit(solution)/shard_map/ppermute | solution.py:495
  6.6 89.4 %collective-permute-start.5 = (bf16[1536,768]{1,0:T(8,128)(2,1)}, bf16[1536,768]{1,0:T(8,128)(2,1)S(1)}, u32[]{:S(2)}, u32[]{:S(2)}) collective-permute-start(bf16[1536,768]{1,0:T(8,128)(2,1)} %down_own.1), channel_id=1, source_target_pairs={{0,1},{1,0},{2,3},{3,2},{4,5},{5,4},{6,7},{7,6},{8,9},{9,8},{10,11... | collective-permute-start | bytes 7077896 | tf_op jit(solution)/shard_map/ppermute | solution.py:495
  46.3 9.6 %collective-permute-start.1 = (bf16[32,32,128]{2,1,0:T(8,128)(2,1)S(1)}, bf16[32,32,128]{2,1,0:T(8,128)(2,1)S(1)}, u32[]{:S(2)}, u32[]{:S(2)}) collective-permute-start(bf16[32,32,128]{2,1,0:T(8,128)(2,1)S(1)} %get-tuple-element.31), channel_id=1, source_target_pairs={{0,2},{2,0},{4,6},{6,4},{8,10},{10,8},{12,14},{14,12},{16,18},{18,... | collective-permute-start | bytes 786440 | tf_op jit(solution)/shard_map/ppermute | solution.py:507
  47.7 48.4 %copy-start.3 = (bf16[1536,768]{1,0:T(8,128)(2,1)S(1)}, bf16[1536,768]{1,0:T(8,128)(2,1)}, u32[]{:S(2)}) copy-start(bf16[1536,768]{1,0:T(8,128)(2,1)} %down_own.1) | copy-start | bytes 7077892
  55.8 40.2 %copy-start.2 = (bf16[768,1536]{1,0:T(8,128)(2,1)S(1)}, bf16[768,1536]{1,0:T(8,128)(2,1)}, u32[]{:S(2)}) copy-start(bf16[768,1536]{1,0:T(8,128)(2,1)} %up_own.1) | copy-start | bytes 7077892
  91.8 4.2 %collective-permute-start.2 = (bf16[64,24,128]{2,1,0:T(8,128)(2,1)S(1)}, bf16[64,24,128]{2,1,0:T(8,128)(2,1)S(1)}, u32[]{:S(2)}, u32[]{:S(2)}) collective-permute-start(bf16[64,24,128]{2,1,0:T(8,128)(2,1)S(1)} %all_to_all.11.g_own), channel_id=1, source_target_pairs={{0,1},{1,0},{2,3},{3,2},{4,5},{5,4},{6,7},{7,6},{8,9},{9,8},{10,11... | collective-permute-start | bytes 1179656 | tf_op jit(solution)/shard_map/ppermute | solution.py:495
  108.8 2.0 %collective-permute-start.6 = (bf16[768,256]{1,0:T(8,128)(2,1)S(1)}, bf16[768,256]{1,0:T(8,128)(2,1)S(1)}, u32[]{:S(2)}, u32[]{:S(2)}) collective-permute-start(bf16[768,256]{1,0:T(8,128)(2,1)S(1)} %get-tuple-element.35.at_own), channel_id=1, source_target_pairs={{0,1},{1,0},{2,3},{3,2},{4,5},{5,4},{6,7},{7,6},{8,9},{9,8},{10,11... | collective-permute-start | bytes 1179656 | tf_op jit(solution)/shard_map/ppermute | solution.py:495
  109.3 1.5 %collective-permute-start.7 = (bf16[256,256]{1,0:T(8,128)(2,1)S(1)}, bf16[256,256]{1,0:T(8,128)(2,1)S(1)}, u32[]{:S(2)}, u32[]{:S(2)}) collective-permute-start(bf16[256,256]{1,0:T(8,128)(2,1)S(1)} %get-tuple-element.36.b_own), channel_id=1, source_target_pairs={{0,1},{1,0},{2,3},{3,2},{4,5},{5,4},{6,7},{7,6},{8,9},{9,8},{10,11... | collective-permute-start | bytes 393224 | tf_op jit(solution)/shard_map/ppermute | solution.py:495

commit v2 on v1

--- a/solution.py
+++ b/solution.py
@@ -322,16 +322,11 @@
     pos_ref, g_own, g_oth, pack_own, pack_oth, small,
     wl_own, wl_oth, up_own, up_oth, down_own, down_oth,
     at_ref, b_ref,
-    enc, mix, wbuf, sem,
+    enc, mix,
 ):
     rows = mix.shape[0]
     head = pos_ref[0]
-    copies = {}
-    for i in (2, 3, 1, 4, 5, 6):
-        for k, (src, at) in enumerate(((wl_own, head), (wl_oth, 1 - head))):
-            dst = wbuf.at[i - 1, pl.ds(pl.multiple_of(at * HALF, HALF), HALF)]
-            copies[i, k] = pltpu.make_async_copy(src.at[i], dst, sem.at[i - 1, k])
-            copies[i, k].start()
+    first = head == 0
     for k, (g, pack) in enumerate(((g_own, pack_own), (g_oth, pack_oth))):
         mean = g[...].astype(f32).reshape(GROUPS, 2, 3, 8, 128)
         for p in range(PAIRS):
@@ -342,9 +337,8 @@
     block_in = norm(enc[...].astype(f32)).astype(bf16)
 
     def proj(x, i):
-        for k in range(2):
-            copies[i, k].wait()
-        return dot(x, wbuf[i - 1])
+        lo, hi = x[:, :HALF], x[:, HALF:]
+        return dot(jnp.where(first, lo, hi), wl_own[i]) + dot(jnp.where(first, hi, lo), wl_oth[i])
 
     keys = proj(block_in, 2).astype(bf16)
     vals = proj(block_in, 3).astype(bf16)
@@ -387,13 +381,11 @@
     return pl.pallas_call(
         latent_kernel,
         out_shape=(shape((WIDTH, rows)), shape((rows, 256))),
-        in_specs=[smem()] + [vmem()] * 5 + [anywhere()] * 2 + [vmem()] * 4,
+        in_specs=[smem()] + [vmem()] * 11,
         out_specs=(vmem(), vmem()),
         scratch_shapes=[
             pltpu.VMEM((2 * rows, WIDTH), bf16),
             pltpu.VMEM((rows, WIDTH), bf16),
-            pltpu.VMEM((6, WIDTH, WIDTH), bf16),
-            pltpu.SemaphoreType.DMA((6, 2)),
         ],
         compiler_params=params(),
         cost_estimate=cost(6 << 30, 20 << 20, 3 << 20),

time: 138 us -> 136 us (0.986)
  Pallas kernels: 90 us -> 88 us
    pallas_call x1, Pallas kernels: 12.7 us -> 11 us  [latent_block(): pl.pallas_call(latent_kernel, out_shape=(shape((WIDTH, rows)), shape((row...]
  transfers between devices with their start and end apart: 8 -> 8, of which waited for: 3 -> 3; matrix products, arithmetic and copies ran while one was open for 0% -> 0% of each run, Pallas kernels for 36% -> 37%
where the time goes in v2:
time: 136 us
  Pallas kernels  88 us (65%)
  blocking collectives  34.4 us (25%)
  starting transfers between devices  7.47 us (5%)
  waiting for transfers between devices  3.09 us (2%)
    pallas_call x1, Pallas kernels, encode(): pl.pallas_call(encode_kernel, out_shape=(shape((GROUPS, 32, 128)), shape(...  39.2 us
    pallas_call x1, Pallas kernels, decode(): pl.pallas_call(decode_kernel, out_shape=shape((16, share), f32), in_specs...  26.9 us
    all_to_all x1, blocking collectives, per_device(): parts = lax.all_to_all(part, 'pts', 0, 0, axis_index_groups=PARITIES)  20.3 us
    all_to_all x1, blocking collectives, per_device(): g_own = lax.all_to_all(merge(parts, OWNERS), 'pts', 0, 0)  14.1 us
    pallas_call x1, Pallas kernels, latent_block(): pl.pallas_call(latent_kernel, out_shape=(shape((WIDTH, rows)), shape((row...  11 us
    pallas_call x1, Pallas kernels, encode_rest(): pl.pallas_call(attend, out_shape=shape((GROUPS, 32, 128)), in_specs=[vmem...  8.17 us
    ppermute x7, starting transfers between devices, other(): return lax.ppermute(x, 'head', swap)  6.07 us
    ppermute x7, waiting for transfers between devices, other(): return lax.ppermute(x, 'head', swap)  3.08 us
  transfers between devices with their start and end apart: 8, of which 3 were waited for; matrix products, arithmetic and copies ran while one was open for 0% of the time, Pallas kernels for 37%

profile of v2, /device:TPU:1, one launch (start us, length us, event | category | flops | bytes accessed | tf_op | source)
XLA Modules:
  0.0 136.2 jit_solution(1401844066146151706)
XLA Ops:
  0.0 1.2 slice_bitcast_fusion
  1.2 0.0 copy-start.1
  1.2 1.2 pad_maximum_fusion.pack_ref.pack_own
  2.4 1.5 %collective-permute-start = (bf16[640,768]{1,0:T(8,128)(2,1)S(1)}, bf16[640,768]{1,0:T(8,128)(2,1)S(1)}, u32[]{:S(2)}, u32[]{:S(2)}) collective-permute-start(bf16[640,768]{1,0:T(8,128)(2,1)S(1)} %pad_maximum_fusion.pack_ref.pack_own), channel_id=1, source_target_pairs={{0,1},{1,0},{2,3},{3,2},{4,5},{5,4},{6,7},{7,6},{8,9},{9,8},{10,11... | collective-permute-start | bytes 2949128 | tf_op jit(solution)/shard_map/ppermute | solution.py:487
  4.6 0.0 copy-done.7
  4.6 0.0 copy-done.4
  4.6 0.0 copy-done.5
  4.7 1.1 prepare.1
  5.8 0.3 collective-permute-done.pack_oth
  6.1 0.4 collective-permute-start.3
  6.5 0.1 collective-permute-start.4
  6.6 0.4 collective-permute-start.5
  7.0 39.2 %encode.1 = (bf16[32,32,128]{2,1,0:T(8,128)(2,1)S(1)}, bf16[1536,128]{1,0:T(8,128)(2,1)S(1)}) custom-call(s32[1]{0:T(128)} %bitcast.pos_ref, s32[1]{0:T(128)} %bitcast.1.par_ref, f32[1]{0:T(128)} %get-tuple-element.24.pn_ref, bf16[256,768]{1,0:T(8,128)(2,1)S(1)} %get-tuple-element.26.normed, bf16[640,768]{1,0:T(8,128)(2,1)S(1)} %pad_maximum_fusion.pack_ref.pack_own, ...), custom_call_target="tpu_custom_call" | custom-call | flops 6442450944 | bytes 6291456 | tf_op jit(solution)/shard_map/encode/pallas_call | solution.py:213
  46.3 1.4 %collective-permute-start.1 = (bf16[32,32,128]{2,1,0:T(8,128)(2,1)S(1)}, bf16[32,32,128]{2,1,0:T(8,128)(2,1)S(1)}, u32[]{:S(2)}, u32[]{:S(2)}) collective-permute-start(bf16[32,32,128]{2,1,0:T(8,128)(2,1)S(1)} %get-tuple-element.31), channel_id=1, source_target_pairs={{0,2},{2,0},{4,6},{6,4},{8,10},{10,8},{12,14},{14,12},{16,18},{18,... | collective-permute-start | bytes 786440 | tf_op jit(solution)/shard_map/ppermute | solution.py:499
  47.7 8.2 %encode_rest.1.x_ref = bf16[32,32,128]{2,1,0:T(8,128)(2,1)S(1)} custom-call(bf16[1536,128]{1,0:T(8,128)(2,1)S(1)} %get-tuple-element.30.q_ref, bf16[128,4096]{1,0:T(8,128)(2,1)S(1)} %get-tuple-element.28.paug, bf16[4096,128]{1,0:T(8,128)(2,1)S(1)} %get-tuple-element.29.pvt), custom_call_target="tpu_custom_call" | custom-call | flops 6442450944 | bytes 6291456 | tf_op jit(solution)/shard_map/encode_rest/pallas_call | solution.py:231
  55.8 0.0 copy-start.2
  55.9 0.0 collective-permute-done.1.y_ref
  55.9 0.9 pair.1
  56.8 20.3 %all_to_all.10.x_ref = bf16[32,32,128]{2,1,0:T(8,128)(2,1)S(1)} all-to-all(bf16[32,32,128]{2,1,0:T(8,128)(2,1)S(1)} %pair.1), channel_id=1, replica_groups={{0,4,8,12,16,20,24,28,32,36,40,44,48,52,56,60,64,68,72,76,80,84,88,92,9..., dimensions={0} | all-to-all | bytes 524288 | tf_op jit(solution)/shard_map/all_to_all | solution.py:502
  77.1 0.7 merge.1
  77.7 14.1 %all_to_all.11.g_own = bf16[64,24,128]{2,1,0:T(8,128)(2,1)S(1)} all-to-all(bf16[64,24,128]{2,1,0:T(8,128)(2,1)S(1)} %merge.1), channel_id=1, replica_groups=mesh['pts'=64,'head'=2] {'pts'}, dimensions={0} | all-to-all | bytes 786432 | tf_op jit(solution)/shard_map/all_to_all | solution.py:503
  91.8 2.9 %collective-permute-start.2 = (bf16[64,24,128]{2,1,0:T(8,128)(2,1)S(1)}, bf16[64,24,128]{2,1,0:T(8,128)(2,1)S(1)}, u32[]{:S(2)}, u32[]{:S(2)}) collective-permute-start(bf16[64,24,128]{2,1,0:T(8,128)(2,1)S(1)} %all_to_all.11.g_own), channel_id=1, source_target_pairs={{0,1},{1,0},{2,3},{3,2},{4,5},{5,4},{6,7},{7,6},{8,9},{9,8},{10,11... | collective-permute-start | bytes 1179656 | tf_op jit(solution)/shard_map/ppermute | solution.py:487
  94.7 1.3 collective-permute-done.2.g_oth
  96.0 0.0 collective-permute-done.4.up_oth
  96.0 0.0 collective-permute-done.5.down_oth
  96.0 0.0 collective-permute-done.3.wl_oth
  96.1 11.0 %latent_block.1 = (bf16[768,256]{1,0:T(8,128)(2,1)S(1)}, bf16[256,256]{1,0:T(8,128)(2,1)S(1)}) custom-call(s32[1]{0:T(128)} %bitcast.pos_ref, bf16[64,24,128]{2,1,0:T(8,128)(2,1)S(1)} %all_to_all.11.g_own, bf16[64,24,128]{2,1,0:T(8,128)(2,1)S(1)} %collective-permute-done.2.g_oth, bf16[640,768]{1,0:T(8,128)(2,1)S(1)} %pad_maximum_fusion.pack_ref.pack_own, ...), custom_call_target="tpu_custom_call" | custom-call | flops 6442450944 | bytes 20971520 | tf_op jit(solution)/shard_map/latent_block/pallas_call | solution.py:381
  107.1 0.7 collective-permute-start.6
  107.7 0.1 collective-permute-start.7
  107.9 1.4 %collective-permute-done.7.b_oth = bf16[256,256]{1,0:T(8,128)(2,1)S(1)} collective-permute-done((bf16[256,256]{1,0:T(8,128)(2,1)S(1)}, bf16[256,256]{1,0:T(8,128)(2,1)S(1)}, u32[]{:S(2)}, u32[]{:S(2)}) %collective-permute-start.7) | collective-permute-done | bytes 131104 | tf_op jit(solution)/shard_map/ppermute | solution.py:487
  109.3 0.0 collective-permute-done.6.at_oth
  109.3 26.9 %decode.1 = f32[16,2048]{1,0:T(8,128)} custom-call(s32[1]{0:T(128)} %bitcast.pos_ref, f32[1]{0:T(128)} %get-tuple-element.24.pn_ref, bf16[64,4096]{1,0:T(8,128)(2,1)S(1)} %copy-done, bf16[768,256]{1,0:T(8,128)(2,1)S(1)} %get-tuple-element.35.at_own, bf16[768,256]{1,0:T(8,128)(2,1)S(1)} %collective-permute-done.6.at_oth, ...), custom_call_target="tpu_custom_call" | custom-call | flops 12884901888 | bytes 8388608 | tf_op jit(solution)/shard_map/decode/pallas_call | solution.py:462
  (12 shorter events, 0.0 us)
Async XLA Ops:
  0.0 4.6 %copy-start.7 = (bf16[768,16]{0,1:T(8,128)(2,1)S(1)}, bf16[768,16]{0,1:T(8,128)(2,1)}, u32[]{:S(2)}) copy-start(bf16[768,16]{0,1:T(8,128)(2,1)} %param.19) | copy-start | bytes 73732
  0.0 4.6 %copy-start.4 = (bf16[64,768]{1,0:T(8,128)(2,1)S(1)}, bf16[64,768]{1,0:T(8,128)(2,1)}, u32[]{:S(2)}) copy-start(bf16[64,768]{1,0:T(8,128)(2,1)} %param.18) | copy-start | bytes 294916
  0.0 4.6 %copy-start.5 = (bf16[64,768]{1,0:T(8,128)(2,1)S(1)}, bf16[64,768]{1,0:T(8,128)(2,1)}, u32[]{:S(2)}) copy-start(bf16[64,768]{1,0:T(8,128)(2,1)} %param.14) | copy-start | bytes 294916
  0.0 4.6 %copy-start.6 = (bf16[64,768]{1,0:T(8,128)(2,1)S(1)}, bf16[64,768]{1,0:T(8,128)(2,1)}, u32[]{:S(2)}) copy-start(bf16[64,768]{1,0:T(8,128)(2,1)} %param.13) | copy-start | bytes 294916
  0.0 4.6 %copy-start = (bf16[64,4096]{1,0:T(8,128)(2,1)S(1)}, bf16[64,4096]{1,0:T(8,128)(2,1)}, u32[]{:S(2)}) copy-start(bf16[64,4096]{1,0:T(8,128)(2,1)} %pts_ref.3) | copy-start | bytes 1572868
  1.2 4.9 %copy-start.1 = (bf16[7,384,768]{2,1,0:T(8,128)(2,1)S(1)}, bf16[7,384,768]{2,1,0:T(8,128)(2,1)}, u32[]{:S(2)}) copy-start(bf16[7,384,768]{2,1,0:T(8,128)(2,1)} %wl_own) | copy-start | bytes 12386308
  2.4 3.7 %collective-permute-start = (bf16[640,768]{1,0:T(8,128)(2,1)S(1)}, bf16[640,768]{1,0:T(8,128)(2,1)S(1)}, u32[]{:S(2)}, u32[]{:S(2)}) collective-permute-start(bf16[640,768]{1,0:T(8,128)(2,1)S(1)} %pad_maximum_fusion.pack_ref.pack_own), channel_id=1, source_target_pairs={{0,1},{1,0},{2,3},{3,2},{4,5},{5,4},{6,7},{7,6},{8,9},{9,8},{10,11... | collective-permute-start | bytes 2949128 | tf_op jit(solution)/shard_map/ppermute | solution.py:487
  6.1 89.9 %collective-permute-start.3 = (bf16[7,384,768]{2,1,0:T(8,128)(2,1)S(1)}, bf16[7,384,768]{2,1,0:T(8,128)(2,1)S(1)}, u32[]{:S(2)}, u32[]{:S(2)}) collective-permute-start(bf16[7,384,768]{2,1,0:T(8,128)(2,1)S(1)} %copy-done.1), channel_id=1, source_target_pairs={{0,1},{1,0},{2,3},{3,2},{4,5},{5,4},{6,7},{7,6},{8,9},{9,8},{10,11... | collective-permute-start | bytes 12386312 | tf_op jit(solution)/shard_map/ppermute | solution.py:487
  6.5 89.5 %collective-permute-start.4 = (bf16[768,1536]{1,0:T(8,128)(2,1)}, bf16[768,1536]{1,0:T(8,128)(2,1)S(1)}, u32[]{:S(2)}, u32[]{:S(2)}) collective-permute-start(bf16[768,1536]{1,0:T(8,128)(2,1)} %up_own.1), channel_id=1, source_target_pairs={{0,1},{1,0},{2,3},{3,2},{4,5},{5,4},{6,7},{7,6},{8,9},{9,8},{10,11... | collective-permute-start | bytes 7077896 | tf_op jit(solution)/shard_map/ppermute | solution.py:487
  6.6 89.4 %collective-permute-start.5 = (bf16[1536,768]{1,0:T(8,128)(2,1)}, bf16[1536,768]{1,0:T(8,128)(2,1)S(1)}, u32[]{:S(2)}, u32[]{:S(2)}) collective-permute-start(bf16[1536,768]{1,0:T(8,128)(2,1)} %down_own.1), channel_id=1, source_target_pairs={{0,1},{1,0},{2,3},{3,2},{4,5},{5,4},{6,7},{7,6},{8,9},{9,8},{10,11... | collective-permute-start | bytes 7077896 | tf_op jit(solution)/shard_map/ppermute | solution.py:487
  46.3 9.6 %collective-permute-start.1 = (bf16[32,32,128]{2,1,0:T(8,128)(2,1)S(1)}, bf16[32,32,128]{2,1,0:T(8,128)(2,1)S(1)}, u32[]{:S(2)}, u32[]{:S(2)}) collective-permute-start(bf16[32,32,128]{2,1,0:T(8,128)(2,1)S(1)} %get-tuple-element.31), channel_id=1, source_target_pairs={{0,2},{2,0},{4,6},{6,4},{8,10},{10,8},{12,14},{14,12},{16,18},{18,... | collective-permute-start | bytes 786440 | tf_op jit(solution)/shard_map/ppermute | solution.py:499
  47.7 48.4 %copy-start.3 = (bf16[1536,768]{1,0:T(8,128)(2,1)S(1)}, bf16[1536,768]{1,0:T(8,128)(2,1)}, u32[]{:S(2)}) copy-start(bf16[1536,768]{1,0:T(8,128)(2,1)} %down_own.1) | copy-start | bytes 7077892
  55.8 40.2 %copy-start.2 = (bf16[768,1536]{1,0:T(8,128)(2,1)S(1)}, bf16[768,1536]{1,0:T(8,128)(2,1)}, u32[]{:S(2)}) copy-start(bf16[768,1536]{1,0:T(8,128)(2,1)} %up_own.1) | copy-start | bytes 7077892
  91.8 4.2 %collective-permute-start.2 = (bf16[64,24,128]{2,1,0:T(8,128)(2,1)S(1)}, bf16[64,24,128]{2,1,0:T(8,128)(2,1)S(1)}, u32[]{:S(2)}, u32[]{:S(2)}) collective-permute-start(bf16[64,24,128]{2,1,0:T(8,128)(2,1)S(1)} %all_to_all.11.g_own), channel_id=1, source_target_pairs={{0,1},{1,0},{2,3},{3,2},{4,5},{5,4},{6,7},{7,6},{8,9},{9,8},{10,11... | collective-permute-start | bytes 1179656 | tf_op jit(solution)/shard_map/ppermute | solution.py:487
  107.1 2.2 %collective-permute-start.6 = (bf16[768,256]{1,0:T(8,128)(2,1)S(1)}, bf16[768,256]{1,0:T(8,128)(2,1)S(1)}, u32[]{:S(2)}, u32[]{:S(2)}) collective-permute-start(bf16[768,256]{1,0:T(8,128)(2,1)S(1)} %get-tuple-element.35.at_own), channel_id=1, source_target_pairs={{0,1},{1,0},{2,3},{3,2},{4,5},{5,4},{6,7},{7,6},{8,9},{9,8},{10,11... | collective-permute-start | bytes 1179656 | tf_op jit(solution)/shard_map/ppermute | solution.py:487
  107.7 1.5 %collective-permute-start.7 = (bf16[256,256]{1,0:T(8,128)(2,1)S(1)}, bf16[256,256]{1,0:T(8,128)(2,1)S(1)}, u32[]{:S(2)}, u32[]{:S(2)}) collective-permute-start(bf16[256,256]{1,0:T(8,128)(2,1)S(1)} %get-tuple-element.36.b_own), channel_id=1, source_target_pairs={{0,1},{1,0},{2,3},{3,2},{4,5},{5,4},{6,7},{7,6},{8,9},{9,8},{10,11... | collective-permute-start | bytes 393224 | tf_op jit(solution)/shard_map/ppermute | solution.py:487
